TPU v7x, 256 devices: a whole 4x4x8 slice. The times are simulated.
256 devices in a mesh: depth: 16 (over z, y_lo), pos: 16 (over x, y_hi, core).
Axes of the slice: x: 4, y: 4 (y_hi: 2, y_lo: 2; y = y_hi * 2 + y_lo), z: 8, core: 2. Of those that a mesh axis runs over, the one named last changes fastest.
Arguments:
- transmission: bfloat16 [32, 2, 512, 512], P('depth', None, 'pos'), may hold values from -1.04 to 1.04, as said below
- probe: bfloat16 [2, 256, 256], replicated, may hold values from -4 to 4
- offsets: int32 [32, 2], P('pos'), may hold values from 0 to 256
- measured: float32 [32, 256, 256], P('pos'), may hold values from 0.25 to 2
Outputs:
- slice_grad: float32 [32, 2, 512, 512], P('depth', None, 'pos')
Inputs may be any that keep to these rules, and one draw needn't show every extreme that they name: `transmission`: each pair of components is a complex number of modulus between 0.96 and 1.04. `offsets`: each position's 256 x 256 window lies inside the 512 x 512 field.
All inputs are finite; a program needn't handle non-finite values.
Results may differ from a plain program's by a relative error of at most 0.035.
Values may be sent and summed in bfloat16 or wider, within the bound.
A program may use at most 64 MiB of HBM per device.

v0:
```python
import functools
import math

import jax
import jax.numpy as jnp
import ml_dtypes
import numpy as np
from jax import lax
from jax.experimental import pallas as pl
from jax.experimental.pallas import tpu as pltpu
from jax.sharding import PartitionSpec as P


MESH = pl.DeviceIdType.MESH
F32 = jnp.float32
BF16 = jnp.bfloat16
VMEM_LIMIT = 56 * 1024 * 1024


def vmem():
    return pl.BlockSpec(memory_space=pltpu.VMEM)


def place():
    d = lax.axis_index("depth")
    q = lax.axis_index("pos")
    return d // 4, d % 4, q // 4, (q // 2) % 2, q % 2


def hi_lo(table, axis):
    high = table.astype(ml_dtypes.bfloat16)
    low = (table - high.astype(np.float64)).astype(ml_dtypes.bfloat16)
    return np.concatenate([high, low], axis)


def right_form(matrix):
    return np.block([[matrix.real, matrix.imag], [-matrix.imag, matrix.real]])


@functools.lru_cache(maxsize=None)
def tables(side):
    half = side // 2
    grid = np.arange(side)
    fourier = np.exp(-2j * np.pi * (np.outer(grid, grid) % side) / side) / math.sqrt(side)
    frequency = (grid + half) % side - half
    phase = np.exp(-1j * math.pi * frequency.astype(np.float64) ** 2 / 1024.0)
    circulant = fourier.conj() @ (phase[:, None] * fourier)
    near, far = circulant[:half, :half], circulant[:half, half:]
    forms = [right_form((near + far) / 2), right_form((near - far) / 2)]
    rights = np.stack([[hi_lo(m, 0) for m in forms], [hi_lo(m.T, 0) for m in forms]])
    order = grid.reshape(2, half // STRIP, STRIP).transpose(1, 0, 2).reshape(side)
    strided = [m[order][:, order] for m in forms]
    lefts = np.stack([[hi_lo(m.T, 1) for m in strided], [hi_lo(m, 1) for m in strided]])
    transforms = np.stack([hi_lo(m, 0) for m in (fourier.real, fourier.imag, -fourier.imag)])
    return rights, lefts, transforms.reshape(3, 2, side, side)


def dot(a, b):
    return jnp.dot(a, b, preferred_element_type=F32)


def cat(parts, axis):
    return jnp.concatenate(parts, axis)


STRIP = 16
BLOCKS = 2


def strips(count):
    return range(0, count, STRIP)


def halves(value):
    middle = value.shape[1] // 2
    return value[:, :middle], value[:, middle:]


def put_sums(ref, at, real, imag):
    (a, b), (c, d) = halves(real), halves(imag)
    ref[0, pl.ds(at, STRIP), :] = cat([a + b, c + d], 1).astype(BF16)
    ref[1, pl.ds(at, STRIP), :] = cat([a - b, c - d], 1).astype(BF16)


def sums_row(row, side):
    half = side // 2
    return 2 * row if row < half else 2 * (row - half) + STRIP


def right_stage(sums, flat, middle, right_ref, way, done=lambda n: None):
    side = sums.shape[1]
    block = side // BLOCKS
    for n in range(BLOCKS):
        for m in range(2):
            x = sums[m, pl.ds(n * block, block), :]
            flat[m, pl.ds(n * block, block), :] = dot(cat([x, x], 1), right_ref[way, m])
        for r in range(n * block, (n + 1) * block, 2 * STRIP):
            s, t = flat[0, pl.ds(r, STRIP), :], flat[0, pl.ds(r + STRIP, STRIP), :]
            d, e = flat[1, pl.ds(r, STRIP), :], flat[1, pl.ds(r + STRIP, STRIP), :]
            for m, (a, b) in enumerate(((s + t, d + e), (s - t, d - e))):
                (a_real, a_imag), (b_real, b_imag) = halves(a), halves(b)
                middle[m, pl.ds(r, STRIP), :] = cat([a_real, b_real], 1).astype(BF16)
                middle[m, pl.ds(r + STRIP, STRIP), :] = cat([a_imag, b_imag], 1).astype(BF16)
        done(n)


def left_stage(middle, field, left_ref, way):
    side = middle.shape[1]
    block = side // BLOCKS
    for n in range(BLOCKS):
        for m in range(2):
            x = middle[m]
            field[m, pl.ds(n * block, block), :] = dot(
                left_ref[way, m, pl.ds(n * block, block), :], cat([x, x], 0)
            )
        for r in range(n * block, (n + 1) * block, 2 * STRIP):
            p, u = field[0, pl.ds(r, STRIP), :], field[0, pl.ds(r + STRIP, STRIP), :]
            m, v = field[1, pl.ds(r, STRIP), :], field[1, pl.ds(r + STRIP, STRIP), :]
            for at, real, imag in ((r // 2, p + m, u + v), (side // 2 + r // 2, p - m, u - v)):
                (a, b), (c, d) = halves(real), halves(imag)
                yield at, cat([a + b, a - b], 1), cat([c + d, c - d], 1)


def strip(ref, s, c, at):
    return ref[s, c, pl.ds(at, STRIP), :].astype(F32)


def fourier_right(real, imag, f, inverse):
    r, i, n = f
    up, down = (n, i) if inverse else (i, n)
    x = cat([real, real, imag, imag], 1)
    a = dot(x, cat([r[0], r[1], down[0], down[1]], 0))
    b = dot(x, cat([up[0], up[1], r[0], r[1]], 0))
    return a, b


def fourier_left(real, imag, f, inverse):
    r, i, n = f
    up, down = (n, i) if inverse else (i, n)
    x = cat([real, real, imag, imag], 0)
    a = dot(cat([r[0], r[1], down[0], down[1]], 1), x)
    b = dot(cat([up[0], up[1], r[0], r[1]], 1), x)
    return a, b


def neighbours(g, j, x, h, core):
    d = 4 * g + j
    xy = 2 * x + h
    partners = [(d, 4 * x + 2 * h + 1 - core)]
    for k in range(1, 8):
        partners.append((d, 2 * ((xy + k) % 8) + core))
    for kx in range(4):
        for kj in range(1, 4):
            partners.append((4 * g + (j + kj) % 4, 4 * ((x + kx) % 4) + 2 * h + core))
    return partners


def remote(src, dst, send, recv, device):
    return pltpu.make_async_remote_copy(
        src_ref=src, dst_ref=dst, send_sem=send, recv_sem=recv, device_id=device, device_id_type=MESH
    )


def one_hot(mask):
    return jnp.where(mask, 1.0, 0.0).astype(BF16)


def shifts(columns):
    return lax.broadcasted_iota(jnp.int32, (STRIP, columns), 1) - lax.broadcasted_iota(
        jnp.int32, (STRIP, columns), 0
    )


def fill_rows(ref, offset):
    rows, columns = ref.shape
    lanes = cat([offset] * (columns // 128), 1)
    base = shifts(columns)
    for r in strips(rows):
        ref[pl.ds(r, STRIP), :] = one_hot(base == lanes + r)


def fill_columns(ref, offset, row_of=lambda r: r):
    rows, columns = ref.shape
    lanes = cat([offset] * (columns // 128), 1)
    base = shifts(columns)
    for r in strips(rows):
        ref[pl.ds(r, STRIP), :] = one_hot(base == row_of(r) - lanes)


def kernel(
    off_ref, t_ref, probe_hbm, measured_hbm, right_hbm, left_hbm, transform_hbm, arrived,
    own_offsets, offs, plane, pick_rows, pick_columns, stage, o_ref, stored, sums, flat, middle, field, grads, measured_ref, right_ref, left_ref,
    transform_ref, patches, put_columns, put_rows, wide, total, partial, sibling_sum, reduced,
    crop_relay, patch_relay, crop_relay_send, crop_relay_recv, patch_relay_send, patch_relay_recv,
    load_sem, s1_send, s1_recv, off_send, off_recv, chip_send, chip_recv, s2_send, s2_recv,
    hop_send, hop_recv, s3_send, s3_recv, back_send, back_recv, s4_send, s4_recv,
):
    g, j, x, h, core = place()
    d = 4 * g + j
    q = 4 * x + 2 * h + core
    xy = 2 * x + h
    last = 3
    sibling = (d, 4 * x + 2 * h + 1 - core)
    win = plane.shape[-1]
    side = o_ref.shape[-1]
    half = side // 2
    count = o_ref.shape[0]
    block = plane.shape[2]
    active = jnp.logical_or(j == core, j == 3 - core)
    mine = jnp.where(j == core, 0, 1)
    ahead = (jnp.minimum(d + 4, 15), q)
    behind = (jnp.maximum(d - 4, 0), q)

    loads = [
        pltpu.make_async_copy(right_hbm, right_ref, load_sem.at[0]),
        pltpu.make_async_copy(left_hbm, left_ref, load_sem.at[1]),
        pltpu.make_async_copy(transform_hbm, transform_ref, load_sem.at[2]),
        pltpu.make_async_copy(measured_hbm.at[mine], measured_ref, load_sem.at[3]),
    ]
    load_probe = pltpu.make_async_copy(probe_hbm, stored.at[0], load_sem.at[4])
    barrier = pltpu.get_barrier_semaphore()
    partners = neighbours(g, j, x, h, core)
    relayed = [(4 * g + (j + k) % 4, 4 * ((x + 1) % 4) + 2 * h + 1 - core) for k in range(4)]
    for partner in partners + relayed:
        pl.semaphore_signal(barrier, inc=1, device_id=partner, device_id_type=MESH)

    @pl.when(jnp.logical_and(active, g < last))
    def _():
        pl.semaphore_signal(barrier, inc=1, device_id=ahead, device_id_type=MESH)

    @pl.when(jnp.logical_and(active, g > 0))
    def _():
        pl.semaphore_signal(barrier, inc=1, device_id=behind, device_id_type=MESH)

    chained = jnp.where(active, jnp.where(jnp.logical_or(g == 0, g == last), 1, 2), 0)
    for load in loads:
        load.start()
    pl.when(g == 0)(load_probe.start)
    for k in range(4):
        own_offsets[k : k + 1, :] = jnp.full((1, 128), off_ref[k // 2, k % 2], jnp.int32)
        own_offsets[k + 4 : k + 5, :] = jnp.zeros((1, 128), jnp.int32)
    pl.semaphore_wait(barrier, len(partners) + len(relayed) + chained)

    for k in range(1, 4):
        to = (x + k) % 4
        remote(
            own_offsets, offs.at[x], off_send.at[k], off_recv.at[k], (d, 4 * to + 2 * h + core)
        ).start()
    for k in (4, 3, 5, 2, 6, 1, 7):
        to = (xy + k) % 8
        tx = to // 2
        remote(
            t_ref.at[tx // 2, tx % 2], plane.at[xy, core], s1_send.at[k], s1_recv.at[k], (d, 2 * to + core)
        ).start()
    own = t_ref.at[x // 2, x % 2]
    remote(own, plane.at[xy, core], chip_send.at[0], chip_recv.at[0], sibling).start()
    plane[xy, core] = t_ref[x // 2, x % 2]
    offs[x] = own_offsets[...]

    for i in (1, 0):
        for k in (0, 3, 2, 1):
            from_x = (x - k + 4) % 4
            if k and i:
                slot = offs.at[from_x]
                remote(slot, slot, off_send.at[k], off_recv.at[k], sibling).wait_recv()
            slot = 2 * ((4 - k) % 4) + i
            fill_rows(pick_rows.at[slot], offs[from_x, 2 * i : 2 * i + 1, :])
            fill_columns(pick_columns.at[slot], offs[from_x, 2 * i + 1 : 2 * i + 2, :])

    for k in (1, 7, 2, 6, 3, 5, 4):
        rows = plane.at[(xy - k + 8) % 8, core]
        remote(rows, rows, s1_send.at[k], s1_recv.at[k], sibling).wait_recv()
        remote(rows, rows, chip_send.at[k], chip_recv.at[k], sibling).start()
    for k in range(8):
        rows = plane.at[(xy - k + 8) % 8, 1 - core]
        remote(rows, rows, chip_send.at[k], chip_recv.at[k], sibling).wait_recv()

    def target(k, i):
        to_j = core if i == 0 else 3 - core
        return to_j, (4 * g + to_j, 4 * ((x + k) % 4) + 2 * h + core)

    own_plane = 2 * j + x // 2
    home = o_ref.at[own_plane, x % 2]
    for i in (1, 0):
        for k in (2, 1, 3, 0):
            slot = 2 * k + i
            rows = dot(pick_rows[slot], plane[...].reshape(win, win)).astype(BF16)
            stage[slot] = dot(rows, pick_columns[slot]).astype(BF16)
            to_j, device = target(k, i)
            copy = remote(
                stage.at[slot], home, s2_send.at[slot], s2_recv.at[2 * own_plane + x % 2], device
            )
            if k == 2:
                pl.when(core == 0)(copy.start)
                pl.when(core == 1)(
                    remote(
                        stage.at[slot], crop_relay.at[i], s2_send.at[slot], crop_relay_recv.at[i],
                        (d, 4 * ((x + 3) % 4) + 2 * h + core),
                    ).start
                )
            elif k:
                copy.start()
            else:
                pl.when(to_j != j)(copy.start)

                @pl.when(to_j == j)
                def _():
                    o_ref[own_plane, x % 2] = stage[slot]

    def crop_forward(i):
        from_x = (x + 1) % 4
        from_plane = 2 * j + from_x // 2
        to_j = core if i == 0 else 3 - core
        return remote(
            crop_relay.at[i], o_ref.at[from_plane, from_x % 2], crop_relay_send.at[i],
            s2_recv.at[2 * from_plane + from_x % 2], (4 * g + to_j, 4 * ((x + 3) % 4) + 2 * h + core),
        )

    @pl.when(core == 1)
    def _():
        for i in (1, 0):
            slot = crop_relay.at[i]
            remote(slot, slot, s2_send.at[0], crop_relay_recv.at[i], sibling).wait_recv()
            crop_forward(i).start()

    for load in loads:
        load.wait()
    pl.when(g == 0)(load_probe.wait)
    half = side // 2
    piece = half // 2

    def forward_pieces(n):
        rows = [pl.ds(m * half + n * piece, piece) for m in range(2)]
        return [
            remote(
                stored.at[count, :, rows[m]], stored.at[0, :, rows[m]],
                hop_send.at[2 * n + m], hop_recv.at[2 * n + m], ahead,
            )
            for m in range(2)
        ]

    def backward_piece(n, device):
        rows = middle.at[:, pl.ds(n * half, half)]
        return remote(rows, rows, hop_send.at[4 + n], hop_recv.at[4 + n], device)

    def owner(s, c):
        return 2 * (s % 2) + c, s // 2

    def make_put_tables():
        for i in range(2):
            for k in range(4):
                at = 4 * (1 - i) + k
                from_x = (x + k) % 4
                fill_rows(put_columns.at[at], offs[from_x, 2 * i + 1 : 2 * i + 2, :])
                for m in range(2):
                    first = 1 - core if m == 0 else core
                    fill_columns(
                        put_rows.at[m, 1 - i, :, k * side : (k + 1) * side],
                        offs[from_x, 2 * i : 2 * i + 1, :],
                        lambda r: r + (r // block + first) * block,
                    )

    starts = jnp.logical_and(active, g == 0)
    pl.when(jnp.logical_not(starts))(make_put_tables)

    @pl.when(active)
    def _():
        def wait_crop(s):
            for c in range(2):
                from_x, from_j = owner(s, c)
                slot = o_ref.at[s, c]
                copy = remote(slot, slot, s2_send.at[0], s2_recv.at[2 * s + c], sibling)
                pl.when(jnp.logical_or(from_x != x, from_j != j))(copy.wait_recv)

        def enter(s, at, real, imag):
            o_real, o_imag = strip(o_ref, s, 0, at), strip(o_ref, s, 1, at)
            put_sums(
                sums, sums_row(at, side), o_real * real - o_imag * imag, o_real * imag + o_imag * real
            )

        def keep_wave(s, at, real, imag):
            stored[s, 0, pl.ds(at, STRIP), :] = real.astype(BF16)
            stored[s, 1, pl.ds(at, STRIP), :] = imag.astype(BF16)

        def forward(s, carry):
            wait_crop(s + 1)
            for at, real, imag in left_stage(middle, field, left_ref, 0):
                keep_wave(s + 1, at, real, imag)
                enter(s + 1, at, real, imag)
            right_stage(sums, flat, middle, right_ref, 0)
            return carry

        wait_crop(0)
        for n in range(2):

            @pl.when(g > 0)
            def _():
                for copy in forward_pieces(n):
                    copy.wait_recv()

            for m in range(2):
                for r in strips(piece):
                    at = m * half + n * piece + r
                    enter(0, at, strip(stored, 0, 0, at), strip(stored, 0, 1, at))
        right_stage(sums, flat, middle, right_ref, 0)
        lax.fori_loop(0, jnp.where(g == last, count - 2, count - 1), forward, 0)

        @pl.when(g < last)
        def _():
            for at, real, imag in left_stage(middle, field, left_ref, 0):
                keep_wave(count, at, real, imag)
                if at >= half and (at + STRIP) % piece == 0:
                    for copy in forward_pieces((at - half) // piece):
                        copy.start()
            pl.when(g == 0)(make_put_tables)
            for n in range(2):
                backward_piece(n, ahead).wait_recv()

        def leave(s, field_strips):
            for at, real, imag in field_strips:
                o_real, o_imag = strip(o_ref, s, 0, at), strip(o_ref, s, 1, at)
                put_sums(
                    sums, sums_row(at, side), o_real * real + o_imag * imag, o_real * imag - o_imag * real
                )
                p_real, p_imag = stored[s, 0, pl.ds(at, STRIP), :], stored[s, 1, pl.ds(at, STRIP), :]
                real, imag = real.astype(BF16), imag.astype(BF16)
                grads[s, 0, pl.ds(at, STRIP), :] = p_real * real + p_imag * imag
                grads[s, 1, pl.ds(at, STRIP), :] = p_real * imag - p_imag * real

        @pl.when(g == last)
        def _():
            final = count - 1
            leaving, turned = grads.at[0], grads.at[1]
            f = [(transform_ref[m, 0], transform_ref[m, 1]) for m in range(3)]

            def flat_strip(m, at):
                return flat[m, pl.ds(at, STRIP), :]

            def transformed(source, inverse):
                turned[0], turned[1] = (v.astype(BF16) for v in fourier_right(source[0], source[1], f, inverse))
                flat[0], flat[1] = fourier_left(turned[0], turned[1], f, inverse)

            wait_crop(final)
            for at, real, imag in left_stage(middle, field, left_ref, 0):
                keep_wave(final, at, real, imag)
                o_real, o_imag = strip(o_ref, final, 0, at), strip(o_ref, final, 1, at)
                leaving[0, pl.ds(at, STRIP), :] = (o_real * real - o_imag * imag).astype(BF16)
                leaving[1, pl.ds(at, STRIP), :] = (o_real * imag + o_imag * real).astype(BF16)
            transformed(leaving, False)
            for at in strips(side):
                real, imag = flat_strip(0, at), flat_strip(1, at)
                weight = real * real + imag * imag - measured_ref[pl.ds(at, STRIP), :]
                sums[0, pl.ds(at, STRIP), :] = (real * weight).astype(BF16)
                sums[1, pl.ds(at, STRIP), :] = (imag * weight).astype(BF16)
            transformed(sums, True)
            leave(final, ((at, flat_strip(0, at), flat_strip(1, at)) for at in strips(side)))
            right_stage(sums, flat, middle, right_ref, 1)

        def send_patches(s):
            for c in range(2):
                to_x, to_j = owner(s, c)
                source, send = grads.at[s, c], s3_send.at[2 * s + c]
                away = jnp.logical_or(to_x != x, to_j != j)
                detour = jnp.logical_and(to_x == (x + 2) % 4, to_j % 2 == 1)
                copy = remote(
                    source, patches.at[2 * x + mine], send, s3_recv.at[2 * x + mine],
                    (4 * g + to_j, 4 * to_x + 2 * h + core),
                )
                pl.when(jnp.logical_and(away, jnp.logical_not(detour)))(copy.start)
                pl.when(detour)(
                    remote(
                        source, patch_relay.at[to_j // 2], send, patch_relay_recv.at[to_j // 2],
                        (d, 4 * ((x + 3) % 4) + 2 * h + 1 - core),
                    ).start
                )

                @pl.when(jnp.logical_not(away))
                def _():
                    patches[2 * x + mine] = grads[s, c]

        def backward(t, carry):
            s = count - 1 - t
            leave(s, left_stage(middle, field, left_ref, 1))
            right_stage(sums, flat, middle, right_ref, 1)
            pl.when(g == 0)(functools.partial(send_patches, s))
            return carry

        lax.fori_loop(jnp.where(g == last, 1, 0), count - 1, backward, 0)
        leave(0, left_stage(middle, field, left_ref, 1))
        pl.when(g == 0)(functools.partial(send_patches, 0))

        @pl.when(g > 0)
        def _():
            def leave_piece(n):
                backward_piece(n, behind).start()

            right_stage(sums, flat, middle, right_ref, 1, leave_piece)
            for n in range(2):
                backward_piece(n, behind).wait_send()

            def send(t, carry):
                send_patches(count - 1 - t)
                return carry

            lax.fori_loop(0, count, send, 0)

    def patch_forward(n):
        from_x = (x + 1) % 4
        p = 2 * from_x + jnp.where(j == 1 - core, 0, 1)
        return remote(
            patch_relay.at[n], patches.at[p], patch_relay_send.at[n], s3_recv.at[p],
            (4 * g + 2 * n + 1, 4 * ((x + 3) % 4) + 2 * h + 1 - core),
        )

    @pl.when(jnp.logical_not(active))
    def _():
        for n in (1, 0):
            slot = patch_relay.at[n]
            remote(slot, slot, s3_send.at[0], patch_relay_recv.at[n], sibling).wait_recv()
            patch_forward(n).start()

    for i in (1, 0):
        group = 1 - i
        for kx in range(4):
            from_x = (x - kx + 4) % 4
            from_j = core if i == 0 else 3 - core
            p = 2 * from_x + i
            slot = patches.at[p]
            copy = remote(slot, slot, s3_send.at[0], s3_recv.at[p], sibling)
            if kx:
                copy.wait_recv()
            else:
                pl.when(from_j != j)(copy.wait_recv)
            at = (4 - kx) % 4
            wide[at * side : (at + 1) * side, :] = dot(slot[...], put_columns[4 * group + at]).astype(BF16)
        if group == 0:
            for m in range(2):
                total[m] = dot(put_rows[m, 0], wide[...])
    partial[...] = (total[0] + dot(put_rows[0, 1], wide[...])).reshape(partial.shape).astype(BF16)
    chip_copy = remote(partial, sibling_sum, back_send.at[0], back_recv.at[0], sibling)
    chip_copy.start()
    own_rows = (total[1] + dot(put_rows[1, 1], wide[...])).reshape(partial.shape)
    chip_copy.wait_recv()
    reduced[...] = (own_rows + sibling_sum[...].astype(F32)).astype(BF16)
    for k in (4, 3, 5, 2, 6, 1, 7):
        to = (xy + k) % 8
        remote(reduced.at[to], arrived.at[4 * h + x], s4_send.at[k], s4_recv.at[k], (d, 2 * to + core)).start()
    arrived[4 * h + x] = reduced[xy]
    for k in range(1, 8):
        come = (xy - k + 8) % 8
        slot = arrived.at[4 * (come % 2) + come // 2]
        remote(slot, slot, s4_send.at[k], s4_recv.at[k], sibling).wait_recv()

    for k in range(1, 8):
        slot = reduced.at[0]
        remote(slot, slot, s1_send.at[k], s1_recv.at[k], sibling).wait_send()
        remote(slot, slot, s4_send.at[k], s4_recv.at[k], sibling).wait_send()
    for k in range(1, 4):
        remote(own_offsets, own_offsets, off_send.at[k], off_recv.at[k], sibling).wait_send()
    for k in range(8):
        slot = reduced.at[0]
        remote(slot, slot, chip_send.at[k], chip_recv.at[k], sibling).wait_send()
    chip_copy.wait_send()
    for i in range(2):
        for k in range(4):
            slot = 2 * k + i
            to_j, device = target(k, i)
            copy = remote(stage.at[slot], home, s2_send.at[slot], s2_recv.at[0], device)
            if k:
                copy.wait_send()
            else:
                pl.when(to_j != j)(copy.wait_send)

    @pl.when(core == 1)
    def _():
        for i in range(2):
            crop_forward(i).wait_send()

    @pl.when(jnp.logical_not(active))
    def _():
        for n in range(2):
            patch_forward(n).wait_send()

    @pl.when(active)
    def _():
        @pl.when(g < last)
        def _():
            for n in range(2):
                for copy in forward_pieces(n):
                    copy.wait_send()

        for s in range(count):
            for c in range(2):
                to_x, to_j = owner(s, c)
                slot = grads.at[s, c]
                copy = remote(slot, slot, s3_send.at[2 * s + c], s3_recv.at[0], sibling)
                pl.when(jnp.logical_or(to_x != x, to_j != j))(copy.wait_send)


def per_device(transmission, probe, offsets, measured):
    layers, _, rows, win = transmission.shape
    side = probe.shape[-1]
    group = 4 * layers
    rights, lefts, transforms = tables(side)
    dma = pltpu.SemaphoreType.DMA
    hbm = pl.BlockSpec(memory_space=pl.ANY)
    smem = pl.BlockSpec(memory_space=pltpu.SMEM)
    arrived = pl.pallas_call(
        kernel,
        out_shape=jax.ShapeDtypeStruct((8, rows, win), BF16),
        in_specs=[smem, vmem(), hbm, hbm, hbm, hbm, hbm],
        out_specs=vmem(),
        scratch_shapes=[
            pltpu.VMEM((8, 128), jnp.int32),
            pltpu.VMEM((4, 8, 128), jnp.int32),
            pltpu.VMEM((8, 2, rows, win), BF16),
            pltpu.VMEM((8, side, win), BF16),
            pltpu.VMEM((8, win, side), BF16),
            pltpu.VMEM((8, side, side), BF16),
            pltpu.VMEM((group, 2, side, side), BF16),
            pltpu.VMEM((group + 1, 2, side, side), BF16),
            pltpu.VMEM((2, side, side), BF16),
            pltpu.VMEM((2, side, side), F32),
            pltpu.VMEM((2, side, side), BF16),
            pltpu.VMEM((2, side, side), F32),
            pltpu.VMEM((group, 2, side, side), BF16),
            pltpu.VMEM((side, side), F32),
            pltpu.VMEM(rights.shape, BF16),
            pltpu.VMEM(lefts.shape, BF16),
            pltpu.VMEM(transforms.shape, BF16),
            pltpu.VMEM((8, side, side), BF16),
            pltpu.VMEM((8, side, win), BF16),
            pltpu.VMEM((2, 2, win // 2, 4 * side), BF16),
            pltpu.VMEM((4 * side, win), BF16),
            pltpu.VMEM((2, win // 2, win), F32),
            pltpu.VMEM((8, rows, win), BF16),
            pltpu.VMEM((8, rows, win), BF16),
            pltpu.VMEM((8, rows, win), BF16),
            pltpu.VMEM((2, side, side), BF16),
            pltpu.VMEM((2, side, side), BF16),
            dma((2,)), dma((2,)), dma((2,)), dma((2,)),
            dma((5,)), dma((8,)), dma((8,)), dma((4,)), dma((4,)), dma((8,)), dma((8,)), dma((8,)),
            dma((16,)), dma((6,)), dma((6,)), dma((16,)), dma((8,)), dma((1,)), dma((1,)), dma((8,)), dma((8,)),
        ],
        compiler_params=pltpu.CompilerParams(
            collective_id=0, has_side_effects=True, vmem_limit_bytes=VMEM_LIMIT
        ),
        name="ptychography_backward",
    )(
        offsets, transmission, probe, measured,
        jnp.asarray(rights), jnp.asarray(lefts), jnp.asarray(transforms),
    )
    parts = arrived.reshape(2, layers, 2, rows, win)
    return parts[0].astype(F32) + parts[1].astype(F32)


def solution(mesh):
    in_specs = (P("depth", None, "pos", None), P(), P("pos", None), P("pos", None, None))
    out_specs = P("depth", None, "pos", None)
    return jax.shard_map(
        per_device, mesh=mesh, in_specs=in_specs, out_specs=out_specs, check_vma=False
    )
```

profile of v0, /device:TPU:1, one launch (start us, length us, event | category | flops | bytes accessed | tf_op | source)
XLA Modules:
  0.0 135.7 jit_solution(14029562051645680222)
XLA Ops:
  0.0 134.0 %ptychography_backward.1 = bf16[8,32,512]{2,1,0:T(8,128)(2,1)} custom-call(s32[2,2]{1,0:T(2,128)} %off_ref.1, bf16[2,2,32,512]{3,2,1,0:T(8,128)(2,1)} %t_ref.1, bf16[2,256,256]{2,1,0:T(8,128)(2,1)} %probe_hbm.1, f32[2,256,256]{2,1,0:T(8,128)} %measured_hbm.1, bf16[2,2,512,256]{3,2,1,0:T(8,128)(2,1)} %constant.6.clone.right_hbm, ...), custom_call_target="tpu_custom_call" | custom-call | tf_op jit(solution)/shard_map/ptychography_backward/pallas_call | solution.py:608
  134.0 1.7 %convert_add_fusion = f32[4,32,512]{2,1,0:T(8,128)} fusion(bf16[8,32,512]{2,1,0:T(8,128)(2,1)} %ptychography_backward.1), kind=kLoop, calls=%fused_computation | loop fusion | flops 196608 | bytes 524288 | tf_op jit(solution)/shard_map/add | solution.py:654
where the time goes:
time: 136 us
  Pallas kernels  134 us (99%)
  other arithmetic  1.7 us (1%)
    pallas_call x1, Pallas kernels, per_device(): pl.pallas_call(kernel, out_shape=jax.ShapeDtypeStruct((8, rows, win), BF1...  134 us

commit v1 on v0

--- a/solution.py
+++ b/solution.py
@@ -188,7 +188,7 @@
 
 
 def kernel(
-    off_ref, t_ref, probe_hbm, measured_hbm, right_hbm, left_hbm, transform_hbm, arrived,
+    off_ref, t_hbm, probe_hbm, measured_hbm, right_hbm, left_hbm, transform_hbm, arrived,
     own_offsets, offs, plane, pick_rows, pick_columns, stage, o_ref, stored, sums, flat, middle, field, grads, measured_ref, right_ref, left_ref,
     transform_ref, patches, put_columns, put_rows, wide, total, partial, sibling_sum, reduced,
     crop_relay, patch_relay, crop_relay_send, crop_relay_recv, patch_relay_send, patch_relay_recv,
@@ -250,11 +250,12 @@
         to = (xy + k) % 8
         tx = to // 2
         remote(
-            t_ref.at[tx // 2, tx % 2], plane.at[xy, core], s1_send.at[k], s1_recv.at[k], (d, 2 * to + core)
+            t_hbm.at[tx // 2, tx % 2], plane.at[xy, core], s1_send.at[k], s1_recv.at[k], (d, 2 * to + core)
         ).start()
-    own = t_ref.at[x // 2, x % 2]
+    own = t_hbm.at[x // 2, x % 2]
     remote(own, plane.at[xy, core], chip_send.at[0], chip_recv.at[0], sibling).start()
-    plane[xy, core] = t_ref[x // 2, x % 2]
+    own_copy = pltpu.make_async_copy(own, plane.at[xy, core], load_sem.at[5])
+    own_copy.start()
     offs[x] = own_offsets[...]
 
     for i in (1, 0):
@@ -274,6 +275,8 @@
     for k in range(8):
         rows = plane.at[(xy - k + 8) % 8, 1 - core]
         remote(rows, rows, chip_send.at[k], chip_recv.at[k], sibling).wait_recv()
+
+    own_copy.wait()
 
     def target(k, i):
         to_j = core if i == 0 else 3 - core
@@ -418,12 +421,12 @@
 
         def leave(s, field_strips):
             for at, real, imag in field_strips:
-                o_real, o_imag = strip(o_ref, s, 0, at), strip(o_ref, s, 1, at)
+                real, imag = real.astype(BF16), imag.astype(BF16)
+                o_real, o_imag = o_ref[s, 0, pl.ds(at, STRIP), :], o_ref[s, 1, pl.ds(at, STRIP), :]
                 put_sums(
                     sums, sums_row(at, side), o_real * real + o_imag * imag, o_real * imag - o_imag * real
                 )
                 p_real, p_imag = stored[s, 0, pl.ds(at, STRIP), :], stored[s, 1, pl.ds(at, STRIP), :]
-                real, imag = real.astype(BF16), imag.astype(BF16)
                 grads[s, 0, pl.ds(at, STRIP), :] = p_real * real + p_imag * imag
                 grads[s, 1, pl.ds(at, STRIP), :] = p_real * imag - p_imag * real
 
@@ -545,11 +548,14 @@
     for k in (4, 3, 5, 2, 6, 1, 7):
         to = (xy + k) % 8
         remote(reduced.at[to], arrived.at[4 * h + x], s4_send.at[k], s4_recv.at[k], (d, 2 * to + core)).start()
-    arrived[4 * h + x] = reduced[xy]
+    kept = pltpu.make_async_copy(reduced.at[xy], arrived.at[4 * h + x], load_sem.at[6])
+    kept.start()
     for k in range(1, 8):
         come = (xy - k + 8) % 8
         slot = arrived.at[4 * (come % 2) + come // 2]
         remote(slot, slot, s4_send.at[k], s4_recv.at[k], sibling).wait_recv()
+
+    kept.wait()
 
     for k in range(1, 8):
         slot = reduced.at[0]
@@ -597,6 +603,14 @@
                 pl.when(jnp.logical_or(to_x != x, to_j != j))(copy.wait_send)
 
 
+def sum_kernel(arrived, out_ref):
+    planes = out_ref.shape[0]
+    for plane in range(planes):
+        for r in strips(out_ref.shape[1]):
+            rows = pl.ds(r, STRIP)
+            out_ref[plane, rows, :] = arrived[plane, rows, :].astype(F32) + arrived[planes + plane, rows, :].astype(F32)
+
+
 def per_device(transmission, probe, offsets, measured):
     layers, _, rows, win = transmission.shape
     side = probe.shape[-1]
@@ -608,8 +622,8 @@
     arrived = pl.pallas_call(
         kernel,
         out_shape=jax.ShapeDtypeStruct((8, rows, win), BF16),
-        in_specs=[smem, vmem(), hbm, hbm, hbm, hbm, hbm],
-        out_specs=vmem(),
+        in_specs=[smem, hbm, hbm, hbm, hbm, hbm, hbm],
+        out_specs=hbm,
         scratch_shapes=[
             pltpu.VMEM((8, 128), jnp.int32),
             pltpu.VMEM((4, 8, 128), jnp.int32),
@@ -639,7 +653,7 @@
             pltpu.VMEM((2, side, side), BF16),
             pltpu.VMEM((2, side, side), BF16),
             dma((2,)), dma((2,)), dma((2,)), dma((2,)),
-            dma((5,)), dma((8,)), dma((8,)), dma((4,)), dma((4,)), dma((8,)), dma((8,)), dma((8,)),
+            dma((7,)), dma((8,)), dma((8,)), dma((4,)), dma((4,)), dma((8,)), dma((8,)), dma((8,)),
             dma((16,)), dma((6,)), dma((6,)), dma((16,)), dma((8,)), dma((1,)), dma((1,)), dma((8,)), dma((8,)),
         ],
         compiler_params=pltpu.CompilerParams(
@@ -650,8 +664,14 @@
         offsets, transmission, probe, measured,
         jnp.asarray(rights), jnp.asarray(lefts), jnp.asarray(transforms),
     )
-    parts = arrived.reshape(2, layers, 2, rows, win)
-    return parts[0].astype(F32) + parts[1].astype(F32)
+    gradient = pl.pallas_call(
+        sum_kernel,
+        out_shape=jax.ShapeDtypeStruct((2 * layers, rows, win), F32),
+        in_specs=[vmem()],
+        out_specs=vmem(),
+        name="sum_halves",
+    )(arrived)
+    return gradient.reshape(layers, 2, rows, win)
 
 
 def solution(mesh):

time: 136 us -> 134 us (0.985)
  other arithmetic: 1.7 us -> 0 us
    add x1 -> x0, other arithmetic: 1.7 us -> none  [per_device(): return parts[0].astype(F32) + parts[1].astype(F32)]
    pallas_call x0 -> x1, Pallas kernels: none -> 1.68 us  [per_device(): pl.pallas_call(sum_kernel, out_shape=jax.ShapeDtypeStruct((2 * layers, ro...]
where the time goes in v1:
time: 134 us
  Pallas kernels  134 us (100%)
    pallas_call x1, Pallas kernels, per_device(): pl.pallas_call(kernel, out_shape=jax.ShapeDtypeStruct((8, rows, win), BF1...  133 us

profile of v1, /device:TPU:1, one launch (start us, length us, event | category | flops | bytes accessed | tf_op | source)
XLA Modules:
  0.0 134.3 jit_solution(8117606681950607421)
XLA Ops:
  0.0 132.6 %ptychography_backward.1.arrived = bf16[8,32,512]{2,1,0:T(8,128)(2,1)} custom-call(s32[2,2]{1,0:T(2,128)} %off_ref.1, bf16[2,2,32,512]{3,2,1,0:T(8,128)(2,1)} %t_hbm.1, bf16[2,256,256]{2,1,0:T(8,128)(2,1)} %probe_hbm.1, f32[2,256,256]{2,1,0:T(8,128)} %measured_hbm.1, bf16[2,2,512,256]{3,2,1,0:T(8,128)(2,1)} %constant.6.clone.right_hbm, ...), custom_call_target="tpu_custom_call" | custom-call | tf_op jit(solution)/shard_map/ptychography_backward/pallas_call | solution.py:622
  132.6 1.7 %sum_halves.1 = f32[4,32,512]{2,1,0:T(8,128)} custom-call(bf16[8,32,512]{2,1,0:T(8,128)(2,1)} %ptychography_backward.1.arrived), custom_call_target="tpu_custom_call" | custom-call | tf_op jit(solution)/shard_map/sum_halves/pallas_call | solution.py:667

commit v2 on v1

--- a/solution.py
+++ b/solution.py
@@ -50,7 +50,12 @@
     rights = np.stack([[hi_lo(m, 0) for m in forms], [hi_lo(m.T, 0) for m in forms]])
     order = grid.reshape(2, half // STRIP, STRIP).transpose(1, 0, 2).reshape(side)
     strided = [m[order][:, order] for m in forms]
-    lefts = np.stack([[hi_lo(m.T, 1) for m in strided], [hi_lo(m, 1) for m in strided]])
+
+    def strip_pairs(table):
+        parts = hi_lo(table, 0).reshape(2, side // STRIP, STRIP, side)
+        return parts.transpose(1, 0, 2, 3).reshape(2 * side, side)
+
+    lefts = np.stack([[strip_pairs(m.T) for m in strided], [strip_pairs(m) for m in strided]])
     transforms = np.stack([hi_lo(m, 0) for m in (fourier.real, fourier.imag, -fourier.imag)])
     return rights, lefts, transforms.reshape(3, 2, side, side)
 
@@ -107,15 +112,17 @@
 def left_stage(middle, field, left_ref, way):
     side = middle.shape[1]
     block = side // BLOCKS
+
+    def total(m, r):
+        return field[m, pl.ds(2 * r, STRIP), :] + field[m, pl.ds(2 * r + STRIP, STRIP), :]
+
     for n in range(BLOCKS):
+        rows = pl.ds(2 * n * block, 2 * block)
         for m in range(2):
-            x = middle[m]
-            field[m, pl.ds(n * block, block), :] = dot(
-                left_ref[way, m, pl.ds(n * block, block), :], cat([x, x], 0)
-            )
+            field[m, rows, :] = dot(left_ref[way, m, rows, :], middle[m])
         for r in range(n * block, (n + 1) * block, 2 * STRIP):
-            p, u = field[0, pl.ds(r, STRIP), :], field[0, pl.ds(r + STRIP, STRIP), :]
-            m, v = field[1, pl.ds(r, STRIP), :], field[1, pl.ds(r + STRIP, STRIP), :]
+            p, u = total(0, r), total(0, r + STRIP)
+            m, v = total(1, r), total(1, r + STRIP)
             for at, real, imag in ((r // 2, p + m, u + v), (side // 2 + r // 2, p - m, u - v)):
                 (a, b), (c, d) = halves(real), halves(imag)
                 yield at, cat([a + b, a - b], 1), cat([c + d, c - d], 1)
@@ -636,7 +643,7 @@
             pltpu.VMEM((2, side, side), BF16),
             pltpu.VMEM((2, side, side), F32),
             pltpu.VMEM((2, side, side), BF16),
-            pltpu.VMEM((2, side, side), F32),
+            pltpu.VMEM((2, 2 * side, side), F32),
             pltpu.VMEM((group, 2, side, side), BF16),
             pltpu.VMEM((side, side), F32),
             pltpu.VMEM(rights.shape, BF16),

time: 134 us -> 132 us (0.985)
  Pallas kernels: 134 us -> 132 us
    pallas_call x1, Pallas kernels: 133 us -> 131 us  [per_device(): pl.pallas_call(kernel, out_shape=jax.ShapeDtypeStruct((8, rows, win), BF1...]
where the time goes in v2:
time: 132 us
  Pallas kernels  132 us (100%)
    pallas_call x1, Pallas kernels, per_device(): pl.pallas_call(kernel, out_shape=jax.ShapeDtypeStruct((8, rows, win), BF1...  131 us

profile of v2, /device:TPU:1, one launch (start us, length us, event | category | flops | bytes accessed | tf_op | source)
XLA Modules:
  0.0 132.2 jit_solution(16396579830705151035)
XLA Ops:
  0.0 130.6 %ptychography_backward.1.arrived = bf16[8,32,512]{2,1,0:T(8,128)(2,1)} custom-call(s32[2,2]{1,0:T(2,128)} %off_ref.1, bf16[2,2,32,512]{3,2,1,0:T(8,128)(2,1)} %t_hbm.1, bf16[2,256,256]{2,1,0:T(8,128)(2,1)} %probe_hbm.1, f32[2,256,256]{2,1,0:T(8,128)} %measured_hbm.1, bf16[2,2,512,256]{3,2,1,0:T(8,128)(2,1)} %constant.6.clone.right_hbm, ...), custom_call_target="tpu_custom_call" | custom-call | tf_op jit(solution)/shard_map/ptychography_backward/pallas_call | solution.py:629
  130.6 1.7 %sum_halves.1 = f32[4,32,512]{2,1,0:T(8,128)} custom-call(bf16[8,32,512]{2,1,0:T(8,128)(2,1)} %ptychography_backward.1.arrived), custom_call_target="tpu_custom_call" | custom-call | tf_op jit(solution)/shard_map/sum_halves/pallas_call | solution.py:674

commit v3 on v2

--- a/solution.py
+++ b/solution.py
@@ -198,7 +198,8 @@
     off_ref, t_hbm, probe_hbm, measured_hbm, right_hbm, left_hbm, transform_hbm, arrived,
     own_offsets, offs, plane, pick_rows, pick_columns, stage, o_ref, stored, sums, flat, middle, field, grads, measured_ref, right_ref, left_ref,
     transform_ref, patches, put_columns, put_rows, wide, total, partial, sibling_sum, reduced,
-    crop_relay, patch_relay, crop_relay_send, crop_relay_recv, patch_relay_send, patch_relay_recv,
+    crop_relay, patch_relay, row_relay, crop_relay_send, crop_relay_recv, patch_relay_send, patch_relay_recv,
+    row_relay_send, row_relay_recv,
     load_sem, s1_send, s1_recv, off_send, off_recv, chip_send, chip_recv, s2_send, s2_recv,
     hop_send, hop_recv, s3_send, s3_recv, back_send, back_recv, s4_send, s4_recv,
 ):
@@ -228,7 +229,11 @@
     barrier = pltpu.get_barrier_semaphore()
     partners = neighbours(g, j, x, h, core)
     relayed = [(4 * g + (j + k) % 4, 4 * ((x + 1) % 4) + 2 * h + 1 - core) for k in range(4)]
-    for partner in partners + relayed:
+    across = 4 * g + j + 1 - 2 * (j % 2)
+    below_h = jnp.where(j % 2 == 1, h, 1 - h)
+    above_h = 1 - below_h
+    above = [(across, 4 * k + 2 * above_h + core) for k in range(4)]
+    for partner in partners + relayed + above:
         pl.semaphore_signal(barrier, inc=1, device_id=partner, device_id_type=MESH)
 
     @pl.when(jnp.logical_and(active, g < last))
@@ -246,19 +251,54 @@
     for k in range(4):
         own_offsets[k : k + 1, :] = jnp.full((1, 128), off_ref[k // 2, k % 2], jnp.int32)
         own_offsets[k + 4 : k + 5, :] = jnp.zeros((1, 128), jnp.int32)
-    pl.semaphore_wait(barrier, len(partners) + len(relayed) + chained)
+    pl.semaphore_wait(barrier, len(partners) + len(relayed) + len(above) + chained)
 
     for k in range(1, 4):
         to = (x + k) % 4
         remote(
             own_offsets, offs.at[x], off_send.at[k], off_recv.at[k], (d, 4 * to + 2 * h + core)
         ).start()
-    for k in (4, 3, 5, 2, 6, 1, 7):
-        to = (xy + k) % 8
-        tx = to // 2
-        remote(
-            t_hbm.at[tx // 2, tx % 2], plane.at[xy, core], s1_send.at[k], s1_recv.at[k], (d, 2 * to + core)
-        ).start()
+    def send_blocks(stage_at, source_of, target_ref, send_sem, recv_sem):
+        for k in (3, 5, 1, 7, 4, 2, 6):
+            to = (xy + k) % 8
+            source = source_of(to)
+            copy = remote(source, target_ref, send_sem.at[k], recv_sem.at[k], (d, 2 * to + core))
+            if k % 2:
+                n = 4 * stage_at + k // 2
+                pl.when(core == 0)(copy.start)
+                pl.when(core == 1)(
+                    remote(
+                        source, row_relay.at[n], send_sem.at[k], row_relay_recv.at[n],
+                        (across, 4 * (to // 2) + 2 * below_h + core),
+                    ).start
+                )
+            else:
+                copy.start()
+
+    def forward_block(stage_at, k, target_of, recv_sem):
+        n = 4 * stage_at + k // 2
+        to = 2 * x + 1 - above_h
+        come = (to - k + 8) % 8
+        return remote(
+            row_relay.at[n], target_of(come), row_relay_send.at[n], recv_sem.at[k], (across, 2 * to + core)
+        )
+
+    def forward_blocks(stage_at, target_of, recv_sem):
+        @pl.when(core == 1)
+        def _():
+            for k in (3, 5, 1, 7):
+                n = 4 * stage_at + k // 2
+                slot = row_relay.at[n]
+                remote(slot, slot, row_relay_send.at[n], row_relay_recv.at[n], sibling).wait_recv()
+                forward_block(stage_at, k, target_of, recv_sem).start()
+
+    def row_slot(come):
+        return plane.at[come, core]
+
+    def sum_slot(come):
+        return arrived.at[4 * (come % 2) + come // 2]
+
+    send_blocks(0, lambda to: t_hbm.at[to // 2 // 2, to // 2 % 2], row_slot(xy), s1_send, s1_recv)
     own = t_hbm.at[x // 2, x % 2]
     remote(own, plane.at[xy, core], chip_send.at[0], chip_recv.at[0], sibling).start()
     own_copy = pltpu.make_async_copy(own, plane.at[xy, core], load_sem.at[5])
@@ -275,7 +315,8 @@
             fill_rows(pick_rows.at[slot], offs[from_x, 2 * i : 2 * i + 1, :])
             fill_columns(pick_columns.at[slot], offs[from_x, 2 * i + 1 : 2 * i + 2, :])
 
-    for k in (1, 7, 2, 6, 3, 5, 4):
+    forward_blocks(0, row_slot, s1_recv)
+    for k in (2, 6, 4, 1, 7, 3, 5):
         rows = plane.at[(xy - k + 8) % 8, core]
         remote(rows, rows, s1_send.at[k], s1_recv.at[k], sibling).wait_recv()
         remote(rows, rows, chip_send.at[k], chip_recv.at[k], sibling).start()
@@ -552,16 +593,13 @@
     own_rows = (total[1] + dot(put_rows[1, 1], wide[...])).reshape(partial.shape)
     chip_copy.wait_recv()
     reduced[...] = (own_rows + sibling_sum[...].astype(F32)).astype(BF16)
-    for k in (4, 3, 5, 2, 6, 1, 7):
-        to = (xy + k) % 8
-        remote(reduced.at[to], arrived.at[4 * h + x], s4_send.at[k], s4_recv.at[k], (d, 2 * to + core)).start()
+    send_blocks(1, lambda to: reduced.at[to], sum_slot(xy), s4_send, s4_recv)
     kept = pltpu.make_async_copy(reduced.at[xy], arrived.at[4 * h + x], load_sem.at[6])
     kept.start()
+    forward_blocks(1, sum_slot, s4_recv)
     for k in range(1, 8):
-        come = (xy - k + 8) % 8
-        slot = arrived.at[4 * (come % 2) + come // 2]
+        slot = sum_slot((xy - k + 8) % 8)
         remote(slot, slot, s4_send.at[k], s4_recv.at[k], sibling).wait_recv()
-
     kept.wait()
 
     for k in range(1, 8):
@@ -588,6 +626,9 @@
     def _():
         for i in range(2):
             crop_forward(i).wait_send()
+        for k in (1, 3, 5, 7):
+            forward_block(0, k, row_slot, s1_recv).wait_send()
+            forward_block(1, k, sum_slot, s4_recv).wait_send()
 
     @pl.when(jnp.logical_not(active))
     def _():
@@ -659,7 +700,8 @@
             pltpu.VMEM((8, rows, win), BF16),
             pltpu.VMEM((2, side, side), BF16),
             pltpu.VMEM((2, side, side), BF16),
-            dma((2,)), dma((2,)), dma((2,)), dma((2,)),
+            pltpu.VMEM((8, rows, win), BF16),
+            dma((2,)), dma((2,)), dma((2,)), dma((2,)), dma((8,)), dma((8,)),
             dma((7,)), dma((8,)), dma((8,)), dma((4,)), dma((4,)), dma((8,)), dma((8,)), dma((8,)),
             dma((16,)), dma((6,)), dma((6,)), dma((16,)), dma((8,)), dma((1,)), dma((1,)), dma((8,)), dma((8,)),
         ],

time: 132 us -> 134 us (1.015)
  Pallas kernels: 132 us -> 134 us
where the time goes in v3:
time: 134 us
  Pallas kernels  134 us (100%)
    pallas_call x1, Pallas kernels, per_device(): pl.pallas_call(kernel, out_shape=jax.ShapeDtypeStruct((8, rows, win), BF1...  132 us

profile of v3, /device:TPU:1, one launch (start us, length us, event | category | flops | bytes accessed | tf_op | source)
XLA Modules:
  0.0 133.6 jit_solution(11791483474513021707)
XLA Ops:
  0.0 131.9 %ptychography_backward.1.arrived = bf16[8,32,512]{2,1,0:T(8,128)(2,1)} custom-call(s32[2,2]{1,0:T(2,128)} %off_ref.1, bf16[2,2,32,512]{3,2,1,0:T(8,128)(2,1)} %t_hbm.1, bf16[2,256,256]{2,1,0:T(8,128)(2,1)} %probe_hbm.1, f32[2,256,256]{2,1,0:T(8,128)} %measured_hbm.1, bf16[2,2,512,256]{3,2,1,0:T(8,128)(2,1)} %constant.6.clone.right_hbm, ...), custom_call_target="tpu_custom_call" | custom-call | tf_op jit(solution)/shard_map/ptychography_backward/pallas_call | solution.py:670
  131.9 1.7 %sum_halves.1 = f32[4,32,512]{2,1,0:T(8,128)} custom-call(bf16[8,32,512]{2,1,0:T(8,128)(2,1)} %ptychography_backward.1.arrived), custom_call_target="tpu_custom_call" | custom-call | tf_op jit(solution)/shard_map/sum_halves/pallas_call | solution.py:716

commit v4 on v2

--- a/solution.py
+++ b/solution.py
@@ -413,10 +413,15 @@
                     at = m * half + n * piece + r
                     enter(0, at, strip(stored, 0, 0, at), strip(stored, 0, 1, at))
         right_stage(sums, flat, middle, right_ref, 0)
-        lax.fori_loop(0, jnp.where(g == last, count - 2, count - 1), forward, 0)
+        def forward_pair(n, carry):
+            forward(2 * n, carry)
+            return forward(2 * n + 1, carry)
+
+        lax.fori_loop(0, (count - 2) // 2, forward_pair, 0)
 
         @pl.when(g < last)
         def _():
+            forward(count - 2, 0)
             for at, real, imag in left_stage(middle, field, left_ref, 0):
                 keep_wave(count, at, real, imag)
                 if at >= half and (at + STRIP) % piece == 0:
@@ -488,14 +493,24 @@
                 def _():
                     patches[2 * x + mine] = grads[s, c]
 
-        def backward(t, carry):
-            s = count - 1 - t
+        def backward(s):
             leave(s, left_stage(middle, field, left_ref, 1))
             right_stage(sums, flat, middle, right_ref, 1)
+
+        def send_pair(s):
             pl.when(g == 0)(functools.partial(send_patches, s))
+            pl.when(g == 0)(functools.partial(send_patches, s - 1))
+
+        def backward_pair(t, carry):
+            s = count - 2 - 2 * t
+            backward(s)
+            backward(s - 1)
+            send_pair(s)
             return carry
 
-        lax.fori_loop(jnp.where(g == last, 1, 0), count - 1, backward, 0)
+        pl.when(g < last)(functools.partial(backward, count - 1))
+        pl.when(g == 0)(functools.partial(send_patches, count - 1))
+        lax.fori_loop(0, (count - 2) // 2, backward_pair, 0)
         leave(0, left_stage(middle, field, left_ref, 1))
         pl.when(g == 0)(functools.partial(send_patches, 0))
 
@@ -531,7 +546,7 @@
 
     for i in (1, 0):
         group = 1 - i
-        for kx in range(4):
+        for kx in (0, 1, 3, 2):
             from_x = (x - kx + 4) % 4
             from_j = core if i == 0 else 3 - core
             p = 2 * from_x + i

time: 132 us -> 132 us (level)
  no operation moved by 1% of the time
where the time goes in v4:
time: 132 us
  Pallas kernels  132 us (100%)
    pallas_call x1, Pallas kernels, per_device(): pl.pallas_call(kernel, out_shape=jax.ShapeDtypeStruct((8, rows, win), BF1...  130 us

profile of v4, /device:TPU:1, one launch (start us, length us, event | category | flops | bytes accessed | tf_op | source)
XLA Modules:
  0.0 131.7 jit_solution(16296205257681368596)
XLA Ops:
  0.0 130.0 %ptychography_backward.1.arrived = bf16[8,32,512]{2,1,0:T(8,128)(2,1)} custom-call(s32[2,2]{1,0:T(2,128)} %off_ref.1, bf16[2,2,32,512]{3,2,1,0:T(8,128)(2,1)} %t_hbm.1, bf16[2,256,256]{2,1,0:T(8,128)(2,1)} %probe_hbm.1, f32[2,256,256]{2,1,0:T(8,128)} %measured_hbm.1, bf16[2,2,512,256]{3,2,1,0:T(8,128)(2,1)} %constant.6.clone.right_hbm, ...), custom_call_target="tpu_custom_call" | custom-call | tf_op jit(solution)/shard_map/ptychography_backward/pallas_call | solution.py:644
  130.1 1.7 %sum_halves.1 = f32[4,32,512]{2,1,0:T(8,128)} custom-call(bf16[8,32,512]{2,1,0:T(8,128)(2,1)} %ptychography_backward.1.arrived), custom_call_target="tpu_custom_call" | custom-call | tf_op jit(solution)/shard_map/sum_halves/pallas_call | solution.py:689

commit v5 on v4

--- a/solution.py
+++ b/solution.py
@@ -98,7 +98,7 @@
     for n in range(BLOCKS):
         for m in range(2):
             x = sums[m, pl.ds(n * block, block), :]
-            flat[m, pl.ds(n * block, block), :] = dot(cat([x, x], 1), right_ref[way, m])
+            flat[m, pl.ds(n * block, block), :] = dot(cat([x, x], 1), right_ref[way, m]).astype(BF16)
         for r in range(n * block, (n + 1) * block, 2 * STRIP):
             s, t = flat[0, pl.ds(r, STRIP), :], flat[0, pl.ds(r + STRIP, STRIP), :]
             d, e = flat[1, pl.ds(r, STRIP), :], flat[1, pl.ds(r + STRIP, STRIP), :]
@@ -448,12 +448,14 @@
             leaving, turned = grads.at[0], grads.at[1]
             f = [(transform_ref[m, 0], transform_ref[m, 1]) for m in range(3)]
 
-            def flat_strip(m, at):
-                return flat[m, pl.ds(at, STRIP), :]
+            def field_strip(m, at):
+                return field[m, pl.ds(at, STRIP), :]
 
             def transformed(source, inverse):
                 turned[0], turned[1] = (v.astype(BF16) for v in fourier_right(source[0], source[1], f, inverse))
-                flat[0], flat[1] = fourier_left(turned[0], turned[1], f, inverse)
+                real, imag = fourier_left(turned[0], turned[1], f, inverse)
+                field[0, :side, :] = real
+                field[1, :side, :] = imag
 
             wait_crop(final)
             for at, real, imag in left_stage(middle, field, left_ref, 0):
@@ -463,12 +465,12 @@
                 leaving[1, pl.ds(at, STRIP), :] = (o_real * imag + o_imag * real).astype(BF16)
             transformed(leaving, False)
             for at in strips(side):
-                real, imag = flat_strip(0, at), flat_strip(1, at)
+                real, imag = field_strip(0, at), field_strip(1, at)
                 weight = real * real + imag * imag - measured_ref[pl.ds(at, STRIP), :]
                 sums[0, pl.ds(at, STRIP), :] = (real * weight).astype(BF16)
                 sums[1, pl.ds(at, STRIP), :] = (imag * weight).astype(BF16)
             transformed(sums, True)
-            leave(final, ((at, flat_strip(0, at), flat_strip(1, at)) for at in strips(side)))
+            leave(final, ((at, field_strip(0, at), field_strip(1, at)) for at in strips(side)))
             right_stage(sums, flat, middle, right_ref, 1)
 
         def send_patches(s):
@@ -656,7 +658,7 @@
             pltpu.VMEM((group, 2, side, side), BF16),
             pltpu.VMEM((group + 1, 2, side, side), BF16),
             pltpu.VMEM((2, side, side), BF16),
-            pltpu.VMEM((2, side, side), F32),
+            pltpu.VMEM((2, side, side), BF16),
             pltpu.VMEM((2, side, side), BF16),
             pltpu.VMEM((2, 2 * side, side), F32),
             pltpu.VMEM((group, 2, side, side), BF16),

time: 132 us -> 132 us (level)
  no operation moved by 1% of the time
where the time goes in v5:
time: 132 us
  Pallas kernels  132 us (100%)
    pallas_call x1, Pallas kernels, per_device(): pl.pallas_call(kernel, out_shape=jax.ShapeDtypeStruct((8, rows, win), BF1...  130 us

profile of v5, /device:TPU:1, one launch (start us, length us, event | category | flops | bytes accessed | tf_op | source)
XLA Modules:
  0.0 131.8 jit_solution(7230521125804001149)
XLA Ops:
  0.0 130.1 %ptychography_backward.1.arrived = bf16[8,32,512]{2,1,0:T(8,128)(2,1)} custom-call(s32[2,2]{1,0:T(2,128)} %off_ref.1, bf16[2,2,32,512]{3,2,1,0:T(8,128)(2,1)} %t_hbm.1, bf16[2,256,256]{2,1,0:T(8,128)(2,1)} %probe_hbm.1, f32[2,256,256]{2,1,0:T(8,128)} %measured_hbm.1, bf16[2,2,512,256]{3,2,1,0:T(8,128)(2,1)} %constant.6.clone.right_hbm, ...), custom_call_target="tpu_custom_call" | custom-call | tf_op jit(solution)/shard_map/ptychography_backward/pallas_call | solution.py:646
  130.1 1.7 %sum_halves.1 = f32[4,32,512]{2,1,0:T(8,128)} custom-call(bf16[8,32,512]{2,1,0:T(8,128)(2,1)} %ptychography_backward.1.arrived), custom_call_target="tpu_custom_call" | custom-call | tf_op jit(solution)/shard_map/sum_halves/pallas_call | solution.py:691

commit v6 on v4

--- a/solution.py
+++ b/solution.py
@@ -300,14 +300,11 @@
             copy = remote(
                 stage.at[slot], home, s2_send.at[slot], s2_recv.at[2 * own_plane + x % 2], device
             )
-            if k == 2:
-                pl.when(core == 0)(copy.start)
-                pl.when(core == 1)(
-                    remote(
-                        stage.at[slot], crop_relay.at[i], s2_send.at[slot], crop_relay_recv.at[i],
-                        (d, 4 * ((x + 3) % 4) + 2 * h + core),
-                    ).start
-                )
+            if k == 2 and i == 1:
+                remote(
+                    stage.at[slot], crop_relay, s2_send.at[slot], crop_relay_recv.at[0],
+                    (d, 4 * ((x + 3) % 4) + 2 * h + core),
+                ).start()
             elif k:
                 copy.start()
             else:
@@ -317,21 +314,13 @@
                 def _():
                     o_ref[own_plane, x % 2] = stage[slot]
 
-    def crop_forward(i):
-        from_x = (x + 1) % 4
-        from_plane = 2 * j + from_x // 2
-        to_j = core if i == 0 else 3 - core
-        return remote(
-            crop_relay.at[i], o_ref.at[from_plane, from_x % 2], crop_relay_send.at[i],
-            s2_recv.at[2 * from_plane + from_x % 2], (4 * g + to_j, 4 * ((x + 3) % 4) + 2 * h + core),
-        )
-
-    @pl.when(core == 1)
-    def _():
-        for i in (1, 0):
-            slot = crop_relay.at[i]
-            remote(slot, slot, s2_send.at[0], crop_relay_recv.at[i], sibling).wait_recv()
-            crop_forward(i).start()
+    from_plane = 2 * j + (x + 1) % 4 // 2
+    crop_forward = remote(
+        crop_relay, o_ref.at[from_plane, (x + 1) % 2], crop_relay_send.at[0],
+        s2_recv.at[2 * from_plane + (x + 1) % 2], (4 * g + 3 - core, 4 * ((x + 3) % 4) + 2 * h + core),
+    )
+    remote(crop_relay, crop_relay, s2_send.at[0], crop_relay_recv.at[0], sibling).wait_recv()
+    crop_forward.start()
 
     for load in loads:
         load.wait()
@@ -599,10 +588,7 @@
             else:
                 pl.when(to_j != j)(copy.wait_send)
 
-    @pl.when(core == 1)
-    def _():
-        for i in range(2):
-            crop_forward(i).wait_send()
+    crop_forward.wait_send()
 
     @pl.when(jnp.logical_not(active))
     def _():
@@ -672,9 +658,9 @@
             pltpu.VMEM((8, rows, win), BF16),
             pltpu.VMEM((8, rows, win), BF16),
             pltpu.VMEM((8, rows, win), BF16),
+            pltpu.VMEM((side, side), BF16),
             pltpu.VMEM((2, side, side), BF16),
-            pltpu.VMEM((2, side, side), BF16),
-            dma((2,)), dma((2,)), dma((2,)), dma((2,)),
+            dma((1,)), dma((1,)), dma((2,)), dma((2,)),
             dma((7,)), dma((8,)), dma((8,)), dma((4,)), dma((4,)), dma((8,)), dma((8,)), dma((8,)),
             dma((16,)), dma((6,)), dma((6,)), dma((16,)), dma((8,)), dma((1,)), dma((1,)), dma((8,)), dma((8,)),
         ],

time: 132 us -> 133 us (level)
  no operation moved by 1% of the time
where the time goes in v6:
time: 133 us
  Pallas kernels  133 us (100%)
    pallas_call x1, Pallas kernels, per_device(): pl.pallas_call(kernel, out_shape=jax.ShapeDtypeStruct((8, rows, win), BF1...  131 us

profile of v6, /device:TPU:1, one launch (start us, length us, event | category | flops | bytes accessed | tf_op | source)
XLA Modules:
  0.0 132.7 jit_solution(7656590421486558838)
XLA Ops:
  0.0 131.0 %ptychography_backward.1.arrived = bf16[8,32,512]{2,1,0:T(8,128)(2,1)} custom-call(s32[2,2]{1,0:T(2,128)} %off_ref.1, bf16[2,2,32,512]{3,2,1,0:T(8,128)(2,1)} %t_hbm.1, bf16[2,256,256]{2,1,0:T(8,128)(2,1)} %probe_hbm.1, f32[2,256,256]{2,1,0:T(8,128)} %measured_hbm.1, bf16[2,2,512,256]{3,2,1,0:T(8,128)(2,1)} %constant.6.clone.right_hbm, ...), custom_call_target="tpu_custom_call" | custom-call | tf_op jit(solution)/shard_map/ptychography_backward/pallas_call | solution.py:630
  131.1 1.7 %sum_halves.1 = f32[4,32,512]{2,1,0:T(8,128)} custom-call(bf16[8,32,512]{2,1,0:T(8,128)(2,1)} %ptychography_backward.1.arrived), custom_call_target="tpu_custom_call" | custom-call | tf_op jit(solution)/shard_map/sum_halves/pallas_call | solution.py:675
